TPU v7x, 32 devices: a whole 2x2x4 slice. The times are simulated.
32 devices in a mesh: inv: 2 (over x), row: 16 (over z, y, core).
Axes of the slice: x: 2, y: 2, z: 4, core: 2. Of those that a mesh axis runs over, the one named last changes fastest.
Arguments:
- rhs_data: float32 [64, 16, 128], P(('inv', 'row')), parts along dimension 0, may hold values from -720 to 720, as said below
- blocks: bfloat16 [12288, 128, 128], P(('inv', 'row')), parts along dimension 0, may hold values from -0.0390625 to 0.0390625
- block_row: int32 [12288], P(('inv', 'row')), parts along dimension 0, may hold values from 0 to 1
- block_col: int32 [12288], P(('inv', 'row')), parts along dimension 0, may hold values from 0 to 31
Outputs:
- model_update: float32 [64, 16, 128], P(('inv', 'row')), parts along dimension 0
- next_search: float32 [64, 16, 128], P(('inv', 'row')), parts along dimension 0
There are 2 independent parts, one for each index of `inv`. A program takes and returns all parts, laid end to end along the dimension named above; each array names one. Nothing has to cross between parts.
Inputs may be any that keep to these rules, and one draw needn't show every extreme that they name: `rhs_data`: each entry is a draw times a row scale, a right-hand side scale and a factor that rises with the data block.
All inputs are finite; a program needn't handle non-finite values.
Results may differ from a plain program's by a relative error of at most 0.0051.
Values may be sent and summed in bfloat16 or wider, within the bound.
A program may use at most 64 MiB of HBM per device.

v0:
```python
import math

import jax
import jax.numpy as jnp
from jax import lax
from jax.sharding import PartitionSpec as P

CB_DEV = 2


epsilon = 1e-06


def local_squares(field):
    return jnp.sum(field * field, axis=(0, 2))


def local(rhs_data, blocks, block_row, block_col):
    db_local = rhs_data.shape[0]
    width = blocks.shape[1]
    count_row = lax.axis_size("row")
    cb_total = CB_DEV * count_row
    norm_data = jnp.sqrt(lax.psum(local_squares(rhs_data), "row") + epsilon)
    data_dir = rhs_data / norm_data[None, :, None]

    def transposed(data_bf):
        picked = data_bf[block_row]
        terms = jnp.einsum("kri,kij->krj", picked, blocks, preferred_element_type=jnp.float32)
        return jnp.zeros((cb_total, picked.shape[1], width), jnp.float32).at[block_col].add(terms)

    partial_value = transposed(data_dir.astype(jnp.bfloat16))
    share = lax.psum_scatter(partial_value, "row", scatter_dimension=0, tiled=True)
    alpha_first = jnp.sqrt(lax.psum(local_squares(share), "row") + epsilon)
    cell_dir = share / alpha_first[None, :, None]
    cell_bf_all = lax.all_gather(cell_dir.astype(jnp.bfloat16), "row", axis=0, tiled=True)
    picked_cells = cell_bf_all[block_col]
    products = jnp.einsum("krj,kij->kri", picked_cells, blocks, preferred_element_type=jnp.float32)
    selector = (block_row[None, :] == jnp.arange(db_local, dtype=jnp.int32)[:, None]).astype(
        jnp.float32
    )
    summed = jnp.einsum("bk,kri->bri", selector, products, precision=lax.Precision.HIGHEST)
    forward = summed - alpha_first[None, :, None] * data_dir
    beta_second = jnp.sqrt(lax.psum(local_squares(forward), "row") + epsilon)
    data_next = forward / beta_second[None, :, None]
    share_next = lax.psum_scatter(
        transposed(data_next.astype(jnp.bfloat16)), "row", scatter_dimension=0, tiled=True
    )
    back_next = share_next - beta_second[None, :, None] * cell_dir
    alpha_second = jnp.sqrt(lax.psum(local_squares(back_next), "row") + epsilon)
    cell_next = back_next / alpha_second[None, :, None]
    rho_value = jnp.sqrt(alpha_first * alpha_first + beta_second * beta_second)
    theta_value = beta_second * alpha_second / rho_value
    phi_value = alpha_first * norm_data / rho_value
    model_update = (phi_value / rho_value)[None, :, None] * cell_dir
    scale = jnp.float32(math.sqrt(float(cb_total * width)))
    next_search = scale * (cell_next - (theta_value / rho_value)[None, :, None] * cell_dir)
    return (model_update, next_search)


def solution(mesh):
    in_specs = (
        P(("inv", "row"), None, None),
        P(("inv", "row"), None, None),
        P(("inv", "row")),
        P(("inv", "row")),
    )
    out_specs = (P(("inv", "row"), None, None), P(("inv", "row"), None, None))
    return jax.shard_map(local, mesh=mesh, in_specs=in_specs, out_specs=out_specs, check_vma=False)
```

profile of v0, /device:TPU:0, one launch (start us, length us, event | category | flops | bytes accessed | tf_op | source)
XLA Modules:
  0.0 332.1 jit_solution(8591314573576703805)
XLA Ops:
  7.2 0.0 reduce-scatter.3.cloned.1.call-start
  7.2 0.8 multiply_reduce_fusion.3
  8.0 34.9 %psum.28 = f32[16]{0:T(128)S(1)} all-reduce(f32[16]{0:T(128)S(1)} %multiply_reduce_fusion.3), channel_id=1, replica_groups=mesh['inv'=2,'row'=16] {'row'}, use_global_device_ids=true, to_apply=%region_1.0 | all-reduce | flops 16 | bytes 128 | tf_op jit(solution)/shard_map/psum | solution.py:23
  43.0 0.8 fusion.5
  43.8 0.7 compare_select_fusion
  44.5 0.7 compare_select_fusion.1
  45.1 2.6 gather_fusion
  47.7 6.8 %fusion.8 = f32[384,16,128]{2,1,0:T(8,128)S(1)} fusion(bf16[384,16,128]{2,1,0:T(8,128)(2,1)} %gather_fusion, bf16[384,128,128]{2,1,0:T(8,128)(2,1)} %param.5), kind=kOutput, calls=%fused_computation.35 | convolution fusion | flops 201326592 | bytes 17301504 | tf_op jit(solution)/shard_map/kri,kij->krj/dot_general | solution.py:28
  54.5 14.6 %scatter_fusion = f32[32,16,128]{2,1,0:T(8,128)S(1)} fusion(f32[32,16,128]{2,1,0:T(8,128)S(1)} %broadcast.22.clone, s32[384]{0:T(512)S(1)} %compare_select_fusion.1, f32[384,16,128]{2,1,0:T(8,128)S(1)} %fusion.8), kind=kCustom, calls=%fused_computation.3 | custom fusion | flops 786432 | bytes 9438720 | tf_op jit(solution)/shard_map/scatter-add | solution.py:29
  69.2 0.0 copy-start.1
  69.2 0.7 copy-done.1
  69.9 0.0 reduce-scatter.3.cloned.1.call-update
  69.9 0.0 reduce-scatter.5.cloned.1.call-start
  70.0 52.7 %reduce-scatter.3.cloned.1.call-done = f32[2,16,128]{2,1,0:T(8,128)} async-done(((f32[32,16,128]{2,1,0:T(8,128)}), f32[2,16,128]{2,1,0:T(8,128)}) %reduce-scatter.3.cloned.1.call-update) | async-done | bytes 16400 | tf_op jit(solution)/shard_map/reduce_scatter | solution.py:32
  122.7 0.8 multiply_reduce_fusion.2
  123.5 29.5 %psum.29 = f32[16]{0:T(128)S(1)} all-reduce(f32[16]{0:T(128)S(1)} %multiply_reduce_fusion.2), channel_id=1, replica_groups=mesh['inv'=2,'row'=16] {'row'}, use_global_device_ids=true, to_apply=%region_5.0 | all-reduce | flops 16 | bytes 128 | tf_op jit(solution)/shard_map/psum | solution.py:33
  153.0 0.8 fusion.7
  153.8 17.5 %all_gather.3 = bf16[32,16,128]{2,1,0:T(8,128)(2,1)S(1)} all-gather(bf16[2,16,128]{2,1,0:T(8,128)(2,1)S(1)} %fusion.7), channel_id=1, replica_groups=mesh['inv'=2,'row'=16] {'row'}, dimensions={0}, use_global_device_ids=true | all-gather | bytes 139264 | tf_op jit(solution)/shard_map/all_gather | solution.py:35
  171.3 1.9 gather_fusion.1
  173.2 0.0 copy-start.4
  173.2 9.1 %fusion.9 = f32[384,16,128]{2,1,0:T(8,128)S(1)} fusion(bf16[384,16,128]{2,1,0:T(8,128)(2,1)S(1)} %gather_fusion.1, bf16[384,128,128]{2,1,0:T(8,128)(2,1)} %param.5), kind=kOutput, calls=%fused_computation.36 | convolution fusion | flops 201326592 | bytes 17301504 | tf_op jit(solution)/shard_map/krj,kij->kri/dot_general | solution.py:37
  182.3 0.0 copy-done.4
  182.3 0.0 copy-start.3
  182.3 2.0 fusion
  184.3 0.0 copy-done.3
  184.3 0.2 multiply_reduce_fusion.1
  184.4 31.4 %psum.30 = f32[16]{0:T(128)S(1)} all-reduce(f32[16]{0:T(128)S(1)} %get-tuple-element.8), channel_id=1, replica_groups=mesh['inv'=2,'row'=16] {'row'}, use_global_device_ids=true, to_apply=%region_7.0 | all-reduce | flops 16 | bytes 128 | tf_op jit(solution)/shard_map/psum | solution.py:43
  215.9 0.1 divide_convert_fusion
  216.0 2.6 gather_fusion.2
  218.5 6.8 %fusion.10 = f32[384,16,128]{2,1,0:T(8,128)S(1)} fusion(bf16[384,16,128]{2,1,0:T(8,128)(2,1)} %gather_fusion.2, bf16[384,128,128]{2,1,0:T(8,128)(2,1)} %param.5), kind=kOutput, calls=%fused_computation.37 | convolution fusion | flops 201326592 | bytes 17301504 | tf_op jit(solution)/shard_map/kri,kij->krj/dot_general | solution.py:28
  225.4 0.0 copy-start.2
  225.4 14.6 %scatter_fusion.1 = f32[32,16,128]{2,1,0:T(8,128)S(1)} fusion(f32[32,16,128]{2,1,0:T(8,128)S(1)} %broadcast.22, s32[384]{0:T(512)S(1)} %compare_select_fusion.1, f32[384,16,128]{2,1,0:T(8,128)S(1)} %fusion.10), kind=kCustom, calls=%fused_computation.4 | custom fusion | flops 786432 | bytes 9438720 | tf_op jit(solution)/shard_map/scatter-add | solution.py:29
  240.0 0.0 copy-start
  240.0 0.7 copy-done
  240.7 0.0 reduce-scatter.5.cloned.1.call-update
  240.7 52.7 %reduce-scatter.5.cloned.1.call-done = f32[2,16,128]{2,1,0:T(8,128)} async-done(((f32[32,16,128]{2,1,0:T(8,128)}), f32[2,16,128]{2,1,0:T(8,128)}) %reduce-scatter.5.cloned.1.call-update) | async-done | bytes 16400 | tf_op jit(solution)/shard_map/reduce_scatter | solution.py:45
  293.5 0.0 copy-done.2
  293.5 0.9 multiply_reduce_fusion
  294.4 29.5 %psum.31 = f32[16]{0:T(128)S(1)} all-reduce(f32[16]{0:T(128)S(1)} %multiply_reduce_fusion), channel_id=1, replica_groups=mesh['inv'=2,'row'=16] {'row'}, use_global_device_ids=true, to_apply=%region_11.0 | all-reduce | flops 16 | bytes 128 | tf_op jit(solution)/shard_map/psum | solution.py:49
  323.9 1.4 subtract_multiply_fusion
  (8 shorter events, 0.1 us)
Async XLA Ops:
  7.2 115.5 %reduce-scatter.3.cloned.1.call-start = ((), (), s32[]{:S(2)}) async-start(), calls=%async_computation.2 | async-start | bytes 278528 | tf_op jit(solution)/shard_map/reduce_scatter | solution.py:32
  69.2 0.7 copy-start.1
  69.9 223.6 %reduce-scatter.5.cloned.1.call-start = ((), (), s32[]{:S(2)}) async-start(), calls=%async_computation.3 | async-start | bytes 278528 | tf_op jit(solution)/shard_map/reduce_scatter | solution.py:45
  173.2 9.1 %copy-start.4 = (s32[384]{0:T(512)S(1)}, s32[384]{0:T(512)}, u32[]{:S(2)}) copy-start(s32[384]{0:T(512)} %param.6) | copy-start | bytes 4612
  182.3 2.0 copy-start.3
  225.4 68.1 %copy-start.2 = (f32[2,16,128]{2,1,0:T(8,128)S(1)}, f32[2,16,128]{2,1,0:T(8,128)}, u32[]{:S(2)}) copy-start(f32[2,16,128]{2,1,0:T(8,128)} %reduce-scatter.3.cloned.1.call-done) | copy-start | bytes 49156
  240.0 0.7 copy-start
Sparse Core Ops, SparseCore 0:
  70.0 52.6 reduce-scatter.2
  240.9 52.5 reduce-scatter.4
where the time goes:
time: 333 us; the launch traced here: 332 us
  blocking collectives  143 us (43%)
  waiting for transfers between devices  106 us (32%)
  other arithmetic  36.6 us (11%)
  matrix products  24.6 us (7%)
  between operations  14.1 us (4%)
  local copies, waits for them, and re-layouts  8.49 us (3%)
    reduce_scatter x1, waiting for transfers between devices, local(): lax.psum_scatter(partial_value, 'row', scatter_dimension=0, tiled=True)  52.7 us
    reduce_scatter x1, waiting for transfers between devices, local(): lax.psum_scatter(transposed(data_next.astype(jnp.bfloat16)), 'row', scatt...  52.7 us
    psum x1, blocking collectives, local(): norm_data = jnp.sqrt(lax.psum(local_squares(rhs_data), 'row') + epsilon)  34.9 us
    psum x1, blocking collectives, local(): beta_second = jnp.sqrt(lax.psum(local_squares(forward), 'row') + epsilon)  31.4 us
    psum x1, blocking collectives, local(): alpha_first = jnp.sqrt(lax.psum(local_squares(share), 'row') + epsilon)  29.5 us
    psum x1, blocking collectives, local(): alpha_second = jnp.sqrt(lax.psum(local_squares(back_next), 'row') + epsilon)  29.5 us
    scatter-add x2, other arithmetic, transposed(): jnp.zeros((cb_total, picked.shape[1], width), jnp.float32).at[block_col]  29.3 us
    all_gather x1, blocking collectives, local(): lax.all_gather(cell_dir.astype(jnp.bfloat16), 'row', axis=0, tiled=True)  17.5 us
  transfers between devices with their start and end apart: 2, of which 2 were waited for; matrix products, arithmetic and copies ran while one was open for 0% of the time, Pallas kernels for 0%

commit v1 on v0

v1 whole, which is shorter than its diff:
```python
import functools
import math

import jax
import jax.numpy as jnp
from jax import lax
from jax.experimental import pallas as pl
from jax.experimental.pallas import tpu as pltpu
from jax.sharding import PartitionSpec as P

CB_DEV = 2
CHUNKS = 8
VMEM_LIMIT = 50 * 1024 * 1024

epsilon = 1e-06
bf16 = jnp.bfloat16
f32 = jnp.float32


def split_two(x):
    high = x.astype(bf16)
    return high, (x - high.astype(f32)).astype(bf16)


def stack_split(x):
    return jnp.concatenate(split_two(x), axis=0)


def row_squares(x):
    return jnp.sum(x * x, axis=-1, keepdims=True)


def spread(s, lanes):
    high = s.astype(bf16).astype(f32)
    rest = s - high
    middle = rest.astype(bf16).astype(f32)
    low = rest - middle
    lane = lax.broadcasted_iota(jnp.int32, (s.shape[0], lanes), 1)
    zero = jnp.zeros((s.shape[0], lanes), f32)
    out = jnp.where(lane == 0, high, zero)
    out = jnp.where(lane == 1, middle, out)
    return jnp.where(lane == 2, low, out).astype(bf16)


def dot(a, b):
    return jnp.dot(a, b, preferred_element_type=f32)


def dot_t(a, b):
    return lax.dot_general(a, b, (((1,), (1,)), ((), ())), preferred_element_type=f32)


def gather_kernel(
    row_ref, col_ref, rhs_ref, blocks_ref, high_ref, low_ref, send_ref,
    held, total, high, low, in_sem, out_sem,
):
    count, width = held.shape[0], held.shape[1]
    db = rhs_ref.shape[0]
    groups = send_ref.shape[0]
    chunk = count // CHUNKS

    def fetch(c):
        span = pl.ds(c * chunk, chunk)
        return pltpu.make_async_copy(blocks_ref.at[span], held.at[span], in_sem.at[c])

    for c in range(CHUNKS):
        fetch(c).start()

    def clear(p, carry):
        total[p] = jnp.zeros((width, width), f32)
        return carry

    lax.fori_loop(0, total.shape[0], clear, 0)

    for c in range(CHUNKS):
        fetch(c).wait()

        def add(k, carry):
            place = col_ref[k] * db + row_ref[k]
            total[place] += held[k].astype(f32)
            return carry

        lax.fori_loop(c * chunk, (c + 1) * chunk, add, 0, unroll=4)

    data = jnp.concatenate([rhs_ref[b] for b in range(db)], axis=-1)
    parts = stack_split(data)
    rows = data.shape[0]
    squares = spread(row_squares(data), width)

    def product(s, carry):
        tops, lows = [], []
        for j in range(CB_DEV):
            cell = s * CB_DEV + j
            strip = jnp.concatenate([total[cell * db + b] for b in range(db)], axis=0)
            top, rest = split_two(strip)
            high[cell] = top
            low[cell] = rest
            tops.append(top)
            lows.append(rest)
        sums = dot(parts, jnp.concatenate(tops, axis=-1)) + dot(parts, jnp.concatenate(lows, axis=-1))
        sums = sums[:rows] + sums[rows:]
        for j in range(CB_DEV):
            send_ref[s, j] = sums[:, j * width:(j + 1) * width].astype(bf16)
        send_ref[s, CB_DEV] = squares
        return carry

    lax.fori_loop(0, groups, product, 0, unroll=2)
    first = pltpu.make_async_copy(high, high_ref, out_sem.at[0])
    second = pltpu.make_async_copy(low, low_ref, out_sem.at[1])
    first.start()
    second.start()
    first.wait()
    second.wait()


def exchange_kernel(
    n, cells_root, send_one, rhs_ref, high_ref, low_ref, model_ref, search_ref,
    high, low, recv_one, send_two, recv_two, send_three, recv_three, send_four, recv_four,
    load_sem, send_sem, recv_sem,
):
    me = lax.axis_index("row")
    width = rhs_ref.shape[2]
    db = rhs_ref.shape[0]
    rows = rhs_ref.shape[1]
    loads = [
        pltpu.make_async_copy(high_ref, high, load_sem.at[0]),
        pltpu.make_async_copy(low_ref, low, load_sem.at[1]),
    ]
    for load in loads:
        load.start()

    barrier = pltpu.get_barrier_semaphore()
    for d in range(1, n):
        pl.semaphore_signal(
            barrier, inc=1, device_id={"row": lax.rem(me + d, n)}, device_id_type=pl.DeviceIdType.MESH
        )
    pl.semaphore_wait(barrier, n - 1)

    def push(phase, d, src, dst):
        return pltpu.make_async_remote_copy(
            src_ref=src,
            dst_ref=dst,
            send_sem=send_sem.at[phase, d],
            recv_sem=recv_sem.at[phase, d],
            device_id={"row": lax.rem(me + d, n)},
            device_id_type=pl.DeviceIdType.MESH,
        )

    def to(d):
        return lax.rem(me + d, n)

    def source(d):
        return lax.rem(me + n - d, n)

    def finish(copies):
        for copy in copies:
            copy.wait_send()

    def cells_of(message):
        return [message[j].astype(f32) for j in range(CB_DEV)]

    def wide(blocks):
        return jnp.concatenate(blocks, axis=-1)

    one = [push(0, d, send_one.at[to(d)], recv_one.at[d]) for d in range(1, n)]
    for copy in one:
        copy.start()
    data = wide([rhs_ref[b] for b in range(db)])
    mine = send_one[me].astype(f32)
    for d in range(1, n):
        one[d - 1].wait_recv()
        mine = mine + recv_one[d].astype(f32)
    beta_one = jnp.sqrt(jnp.sum(mine[CB_DEV], axis=-1, keepdims=True) + epsilon)
    back_one = wide([mine[j] for j in range(CB_DEV)]) / beta_one

    back_bf = back_one.astype(bf16)
    for j in range(CB_DEV):
        send_two[j] = back_bf[:, j * width:(j + 1) * width]
    send_two[CB_DEV] = spread(row_squares(back_one), width)
    two = [push(1, d, send_two, recv_two.at[d]) for d in range(1, n)]
    for copy in two:
        copy.start()
    for load in loads:
        load.wait()

    def strip(ref, s):
        return wide([ref[s * CB_DEV + j] for j in range(CB_DEV)])

    forward = dot_t(back_bf, strip(high, me)) + dot_t(back_bf, strip(low, me))
    squares = send_two[CB_DEV].astype(f32)
    for d in range(1, n):
        two[d - 1].wait_recv()
        s = source(d)
        cells = wide([recv_two[d, j] for j in range(CB_DEV)])
        forward = forward + dot_t(cells, strip(high, s)) + dot_t(cells, strip(low, s))
        squares = squares + recv_two[d, CB_DEV].astype(f32)
    alpha_one = jnp.sqrt(jnp.sum(squares, axis=-1, keepdims=True) + epsilon)
    forward = forward / alpha_one - alpha_one * (data / beta_one)

    parts = stack_split(forward)
    own_squares = spread(row_squares(forward), width)

    def terms(s):
        sums = dot(parts, strip(high, s)) + dot(parts, strip(low, s))
        return sums[:rows] + sums[rows:]

    three = []
    for d in range(1, n):
        sums = terms(to(d)).astype(bf16)
        for j in range(CB_DEV):
            send_three[d, j] = sums[:, j * width:(j + 1) * width]
        send_three[d, CB_DEV] = own_squares
        copy = push(2, d, send_three.at[d], recv_three.at[d])
        copy.start()
        three.append(copy)
    back = terms(me)
    squares = own_squares.astype(f32)
    for d in range(1, n):
        three[d - 1].wait_recv()
        back = back + wide([recv_three[d, j].astype(f32) for j in range(CB_DEV)])
        squares = squares + recv_three[d, CB_DEV].astype(f32)
    beta_two = jnp.sqrt(jnp.sum(squares, axis=-1, keepdims=True) + epsilon)
    cell_dir = back_one / alpha_one
    back_two = back / beta_two - beta_two * cell_dir

    last = row_squares(back_two)
    lane = lax.broadcasted_iota(jnp.int32, (rows // 2, width), 1)
    send_four[...] = jnp.where(
        lane == 0, last[: rows // 2], jnp.where(lane == 1, last[rows // 2:], jnp.zeros((rows // 2, width), f32))
    )
    four = [push(3, d, send_four, recv_four.at[d]) for d in range(1, n)]
    for copy in four:
        copy.start()
    rho = jnp.sqrt(alpha_one * alpha_one + beta_two * beta_two)
    phi = alpha_one * beta_one / rho
    model = (phi / rho) * cell_dir
    for j in range(CB_DEV):
        model_ref[j] = model[:, j * width:(j + 1) * width]
    finish(one)
    finish(two)
    finish(three)
    sums = send_four[...]
    for d in range(1, n):
        four[d - 1].wait_recv()
        sums = sums + recv_four[d]
    alpha_two = jnp.sqrt(jnp.concatenate([sums[:, 0:1], sums[:, 1:2]], axis=0) + epsilon)
    cell_next = back_two / alpha_two
    theta = beta_two * alpha_two / rho
    search = cells_root * (cell_next - (theta / rho) * cell_dir)
    for j in range(CB_DEV):
        search_ref[j] = search[:, j * width:(j + 1) * width]
    finish(four)


def local(rhs_data, blocks, block_row, block_col):
    n = lax.axis_size("row")
    db, rows, width = rhs_data.shape
    count = blocks.shape[0]
    cells = CB_DEV * n
    vmem = pl.BlockSpec(memory_space=pltpu.VMEM)
    smem = pl.BlockSpec(memory_space=pltpu.SMEM)
    anywhere = pl.BlockSpec(memory_space=pl.ANY)
    strip = (cells, db * width, width)
    message = (CB_DEV + 1, rows, width)
    high, low, send_one = pl.pallas_call(
        gather_kernel,
        out_shape=(
            jax.ShapeDtypeStruct(strip, bf16),
            jax.ShapeDtypeStruct(strip, bf16),
            jax.ShapeDtypeStruct((n,) + message, bf16),
        ),
        in_specs=[smem, smem, vmem, anywhere],
        out_specs=(anywhere, anywhere, vmem),
        scratch_shapes=[
            pltpu.VMEM((count, width, width), bf16),
            pltpu.VMEM((cells * db, width, width), f32),
            pltpu.VMEM(strip, bf16),
            pltpu.VMEM(strip, bf16),
            pltpu.SemaphoreType.DMA((CHUNKS,)),
            pltpu.SemaphoreType.DMA((2,)),
        ],
        compiler_params=pltpu.CompilerParams(vmem_limit_bytes=VMEM_LIMIT),
        name="strip",
    )(block_row, block_col, rhs_data, blocks)
    out = jax.ShapeDtypeStruct((CB_DEV, rows, width), f32)
    return pl.pallas_call(
        functools.partial(exchange_kernel, n, math.sqrt(float(cells * width))),
        out_shape=(out, out),
        in_specs=[vmem, vmem, anywhere, anywhere],
        out_specs=(vmem, vmem),
        scratch_shapes=[
            pltpu.VMEM(strip, bf16),
            pltpu.VMEM(strip, bf16),
            pltpu.VMEM((n,) + message, bf16),
            pltpu.VMEM(message, bf16),
            pltpu.VMEM((n,) + message, bf16),
            pltpu.VMEM((n,) + message, bf16),
            pltpu.VMEM((n,) + message, bf16),
            pltpu.VMEM((rows // 2, width), f32),
            pltpu.VMEM((n, rows // 2, width), f32),
            pltpu.SemaphoreType.DMA((2,)),
            pltpu.SemaphoreType.DMA((4, n)),
            pltpu.SemaphoreType.DMA((4, n)),
        ],
        compiler_params=pltpu.CompilerParams(
            collective_id=0, has_side_effects=True, vmem_limit_bytes=VMEM_LIMIT
        ),
        name="exchange",
    )(send_one, rhs_data, high, low)


def solution(mesh):
    in_specs = (
        P(("inv", "row"), None, None),
        P(("inv", "row"), None, None),
        P(("inv", "row")),
        P(("inv", "row")),
    )
    out_specs = (P(("inv", "row"), None, None), P(("inv", "row"), None, None))
    return jax.shard_map(local, mesh=mesh, in_specs=in_specs, out_specs=out_specs, check_vma=False)
```

time: 333 us -> 45.6 us (0.14)
  blocking collectives: 143 us -> 0 us
  waiting for transfers between devices: 106 us -> 0 us
  Pallas kernels: 0 us -> 41.3 us
  other arithmetic: 36.6 us -> 0 us
  matrix products: 24.6 us -> 0 us
  between operations: 14.1 us -> 0.66 us
  local copies, waits for them, and re-layouts: 8.49 us -> 3.29 us
    psum x4 -> x0, blocking collectives: 125 us -> none  [the longest x1 34.9 us: local(): norm_data = jnp.sqrt(lax.psum(local_squares(rhs_data), 'row') + epsilon)]
    reduce_scatter x2 -> x0, waiting for transfers between devices: 105 us -> none  [the longest x1 52.7 us: local(): lax.psum_scatter(partial_value, 'row', scatter_dimension=0, tiled=True)]
    pallas_call x0 -> x2, Pallas kernels: none -> 41.3 us  [the longest x1 32.3 us: local(): pl.pallas_call(functools.partial(exchange_kernel, n, math.sqrt(float(cell...]
    scatter-add x2 -> x0, other arithmetic: 29.3 us -> none  [transposed(): jnp.zeros((cb_total, picked.shape[1], width), jnp.float32).at[block_col]]
    dot_general x4 -> x0, matrix products: 24.6 us -> none  [the longest x2 13.6 us: transposed(): jnp.einsum('kri,kij->krj', picked, blocks, preferred_element_type=jnp.flo...]
    all_gather x1 -> x0, blocking collectives: 17.5 us -> none  [local(): lax.all_gather(cell_dir.astype(jnp.bfloat16), 'row', axis=0, tiled=True)]
    gather x3 -> x0, local copies, waits for them, and re-layouts: 7.04 us -> none  [the longest x2 5.13 us: transposed(): picked = data_bf[block_row]]
  transfers between devices with their start and end apart: 2 -> 0, of which waited for: 2 -> 0; matrix products, arithmetic and copies ran while one was open for 0% -> 0% of each run, Pallas kernels for 0% -> 0%
where the time goes in v1:
time: 45.6 us; the launch traced here: 45.3 us
  Pallas kernels  41.3 us (91%)
  local copies, waits for them, and re-layouts  3.29 us (7%)
  between operations  0.66 us (1%)
    pallas_call x1, Pallas kernels, local(): pl.pallas_call(functools.partial(exchange_kernel, n, math.sqrt(float(cell...  32.3 us
    pallas_call x1, Pallas kernels, local(): pl.pallas_call(gather_kernel, out_shape=(jax.ShapeDtypeStruct(strip, bf16...  9.01 us
    unnamed x8, local copies, waits for them, and re-layouts  3.29 us

profile of v1, /device:TPU:0, one launch (start us, length us, event | category | flops | bytes accessed | tf_op | source)
XLA Modules:
  0.0 45.3 jit_solution(15443192765476354370)
XLA Ops:
  0.6 0.0 copy-start
  0.6 0.7 %copy-done = f32[2,16,128]{2,1,0:T(8,128)S(1)} copy-done((f32[2,16,128]{2,1,0:T(8,128)S(1)}, f32[2,16,128]{2,1,0:T(8,128)}, u32[]{:S(2)}) %copy-start) | copy-done | bytes 16408
  1.3 0.0 copy-start.1
  1.4 0.7 %copy-done.1 = s32[384]{0:T(512)S(1)} copy-done((s32[384]{0:T(512)S(1)}, s32[384]{0:T(512)}, u32[]{:S(2)}) %copy-start.1) | copy-done | bytes 1560
  2.0 0.0 copy-start.2
  2.0 0.7 %copy-done.2 = s32[384]{0:T(512)S(1)} copy-done((s32[384]{0:T(512)S(1)}, s32[384]{0:T(512)}, u32[]{:S(2)}) %copy-start.2) | copy-done | bytes 1560
  2.7 9.0 %strip.1 = (bf16[32,256,128]{2,1,0:T(8,128)(2,1)S(1)}, bf16[32,256,128]{2,1,0:T(8,128)(2,1)}, bf16[16,3,16,128]{3,2,1,0:T(8,128)(2,1)S(1)}) custom-call(s32[384]{0:T(512)S(1)} %copy-done.1, s32[384]{0:T(512)S(1)} %copy-done.2, f32[2,16,128]{2,1,0:T(8,128)S(1)} %copy-done, bf16[384,128,128]{2,1,0:T(8,128)(2,1)} %blocks_ref.1), custom_call_target="tpu_custom_call" | custom-call | tf_op jit(solution)/shard_map/strip/pallas_call | solution.py:265
  11.7 32.3 %exchange.1 = (f32[2,16,128]{2,1,0:T(8,128)S(1)}, f32[2,16,128]{2,1,0:T(8,128)S(1)}) custom-call(bf16[16,3,16,128]{3,2,1,0:T(8,128)(2,1)S(1)} %get-tuple-element.5.send_one, f32[2,16,128]{2,1,0:T(8,128)S(1)} %copy-done, bf16[32,256,128]{2,1,0:T(8,128)(2,1)S(1)} %get-tuple-element.6.high_ref, bf16[32,256,128]{2,1,0:T(8,128)(2,1)} %get-tuple-element.7.low_ref), custom_call_target="tpu_custom_call" | custom-call | tf_op jit(solution)/shard_map/exchange/pallas_call | solution.py:286
  44.1 0.6 %copy.8 = f32[2,16,128]{2,1,0:T(8,128)} copy(f32[2,16,128]{2,1,0:T(8,128)S(1)} %get-tuple-element.10) | data formatting | bytes 32768
  44.7 0.6 %copy.9 = f32[2,16,128]{2,1,0:T(8,128)} copy(f32[2,16,128]{2,1,0:T(8,128)S(1)} %get-tuple-element.11) | data formatting | bytes 32768
Async XLA Ops:
  0.6 0.7 %copy-start = (f32[2,16,128]{2,1,0:T(8,128)S(1)}, f32[2,16,128]{2,1,0:T(8,128)}, u32[]{:S(2)}) copy-start(f32[2,16,128]{2,1,0:T(8,128)} %rhs_ref.3) | copy-start | bytes 49156
  1.3 0.7 %copy-start.1 = (s32[384]{0:T(512)S(1)}, s32[384]{0:T(512)}, u32[]{:S(2)}) copy-start(s32[384]{0:T(512)} %row_ref.1) | copy-start | bytes 4612
  2.0 0.7 %copy-start.2 = (s32[384]{0:T(512)S(1)}, s32[384]{0:T(512)}, u32[]{:S(2)}) copy-start(s32[384]{0:T(512)} %col_ref.1) | copy-start | bytes 4612

commit v2 on v1

v2 whole, which is shorter than its diff:
```python
import functools
import math

import jax
import jax.numpy as jnp
from jax import lax
from jax.experimental import pallas as pl
from jax.experimental.pallas import tpu as pltpu
from jax.sharding import PartitionSpec as P

CB_DEV = 2
CHUNKS = 16
SPARE = 4 * 1024 * 1024
LEAST = 46 * 1024 * 1024

epsilon = 1e-06
bf16 = jnp.bfloat16
f32 = jnp.float32


def split_two(x):
    high = x.astype(bf16)
    return high, (x - high.astype(f32)).astype(bf16)


def stack_split(x):
    return jnp.concatenate(split_two(x), axis=0)


def row_squares(x):
    return jnp.sum(x * x, axis=-1, keepdims=True)


def diagonal(rows, lanes):
    row = lax.broadcasted_iota(jnp.int32, (rows, lanes), 0)
    return row == lax.broadcasted_iota(jnp.int32, (rows, lanes), 1)


def to_lanes(column, lanes):
    shape = (column.shape[0], lanes)
    placed = jnp.where(diagonal(*shape), jnp.broadcast_to(column, shape), 0.0)
    return jnp.sum(placed, axis=0, keepdims=True)


def from_lanes(line, rows):
    shape = (rows, line.shape[1])
    placed = jnp.where(diagonal(*shape), jnp.broadcast_to(line, shape), 0.0)
    return jnp.sum(placed, axis=1, keepdims=True)


def dot(a, b):
    return jnp.dot(a, b, preferred_element_type=f32)


def dot_t(a, b):
    return lax.dot_general(a, b, (((1,), (1,)), ((), ())), preferred_element_type=f32)


def gather_kernel(
    place_hbm, rhs_hbm, blocks_ref, high, low, send_ref,
    place_ref, rhs_ref, held, total, small_sem, in_sem,
):
    count, width = held.shape[0], held.shape[1]
    db = rhs_ref.shape[0]
    groups = send_ref.shape[0]
    chunk = count // CHUNKS

    def fetch(c):
        span = pl.ds(c * chunk, chunk)
        return pltpu.make_async_copy(blocks_ref.at[span], held.at[span], in_sem.at[c])

    small = [
        pltpu.make_async_copy(place_hbm, place_ref, small_sem.at[0]),
        pltpu.make_async_copy(rhs_hbm, rhs_ref, small_sem.at[1]),
    ]
    for copy in small:
        copy.start()
    for c in range(CHUNKS):
        fetch(c).start()

    def clear(p, carry):
        total[p] = jnp.zeros((width, width), f32)
        return carry

    lax.fori_loop(0, total.shape[0], clear, 0)
    for copy in small:
        copy.wait()

    for c in range(CHUNKS):
        fetch(c).wait()

        def add(k, carry):
            total[place_ref[k]] += held[k].astype(f32)
            return carry

        lax.fori_loop(c * chunk, (c + 1) * chunk, add, 0, unroll=4)

    data = jnp.concatenate([rhs_ref[b] for b in range(db)], axis=-1)
    parts = stack_split(data)
    rows = data.shape[0]

    def product(s, carry):
        tops, lows = [], []
        for j in range(CB_DEV):
            cell = s * CB_DEV + j
            strip = jnp.concatenate([total[cell * db + b] for b in range(db)], axis=0)
            top, rest = split_two(strip)
            high[cell] = top
            low[cell] = rest
            tops.append(top)
            lows.append(rest)
        sums = dot(parts, jnp.concatenate(tops, axis=-1)) + dot(parts, jnp.concatenate(lows, axis=-1))
        sums = sums[:rows] + sums[rows:]
        for j in range(CB_DEV):
            send_ref[s, j] = sums[:, j * width:(j + 1) * width].astype(bf16)
        return carry

    lax.fori_loop(0, groups, product, 0, unroll=2)


def exchange_kernel(
    n, cells_root, send_one, rhs_hbm, high, low, model_ref, search_ref,
    rhs_ref, recv_one, send_two, recv_two, send_three, recv_three, send_sums, recv_sums,
    load_sem, send_sem, recv_sem, send_sum_sem, recv_sum_sem,
):
    me = lax.axis_index("row")
    width = rhs_ref.shape[2]
    db = rhs_ref.shape[0]
    rows = rhs_ref.shape[1]
    small = pltpu.make_async_copy(rhs_hbm, rhs_ref, load_sem)
    small.start()
    barrier = pltpu.get_barrier_semaphore()
    for d in range(1, n):
        pl.semaphore_signal(
            barrier, inc=1, device_id={"row": lax.rem(me + d, n)}, device_id_type=pl.DeviceIdType.MESH
        )
    pl.semaphore_wait(barrier, n - 1)

    def push(phase, d, src, dst):
        return pltpu.make_async_remote_copy(
            src_ref=src,
            dst_ref=dst,
            send_sem=send_sem.at[phase, d],
            recv_sem=recv_sem.at[phase, d],
            device_id={"row": lax.rem(me + d, n)},
            device_id_type=pl.DeviceIdType.MESH,
        )

    def push_sums(phase, d):
        return pltpu.make_async_remote_copy(
            src_ref=send_sums.at[phase],
            dst_ref=recv_sums.at[phase, d],
            send_sem=send_sum_sem.at[phase, d],
            recv_sem=recv_sum_sem.at[phase, d],
            device_id={"row": lax.rem(me + d, n)},
            device_id_type=pl.DeviceIdType.MESH,
        )

    def start_sums(phase, column):
        send_sums[phase] = to_lanes(column, width)
        copies = [push_sums(phase, d) for d in range(1, n)]
        for copy in copies:
            copy.start()
        return copies

    def end_sums(phase, copies):
        line = send_sums[phase]
        for d in range(1, n):
            copies[d - 1].wait_recv()
            line = line + recv_sums[phase, d]
        return from_lanes(line, rows)

    def to(d):
        return lax.rem(me + d, n)

    def source(d):
        return lax.rem(me + n - d, n)

    def finish(copies):
        for copy in copies:
            copy.wait_send()

    def wide(blocks):
        return jnp.concatenate(blocks, axis=-1)

    one = [push(0, d, send_one.at[to(d)], recv_one.at[d]) for d in range(1, n)]
    for copy in one:
        copy.start()
    small.wait()
    data = wide([rhs_ref[b] for b in range(db)])
    sums_one = start_sums(0, row_squares(data))
    mine = send_one[me].astype(f32)
    for d in range(1, n):
        one[d - 1].wait_recv()
        mine = mine + recv_one[d].astype(f32)
    beta_one = jnp.sqrt(end_sums(0, sums_one) + epsilon)
    back_one = wide([mine[j] for j in range(CB_DEV)]) / beta_one

    back_bf = back_one.astype(bf16)
    for j in range(CB_DEV):
        send_two[j] = back_bf[:, j * width:(j + 1) * width]
    two = [push(1, d, send_two, recv_two.at[d]) for d in range(1, n)]
    for copy in two:
        copy.start()
    sums_two = start_sums(1, row_squares(back_one))

    def strip(ref, s):
        return wide([ref[s * CB_DEV + j] for j in range(CB_DEV)])

    forward = dot_t(back_bf, strip(high, me)) + dot_t(back_bf, strip(low, me))
    for d in range(1, n):
        two[d - 1].wait_recv()
        s = source(d)
        cells = wide([recv_two[d, j] for j in range(CB_DEV)])
        forward = forward + dot_t(cells, strip(high, s)) + dot_t(cells, strip(low, s))
    alpha_one = jnp.sqrt(end_sums(1, sums_two) + epsilon)
    forward = forward / alpha_one - alpha_one * (data / beta_one)

    parts = stack_split(forward)

    def terms(s):
        sums = dot(parts, strip(high, s)) + dot(parts, strip(low, s))
        return sums[:rows] + sums[rows:]

    three = []
    for d in range(1, n):
        sums = terms(to(d)).astype(bf16)
        for j in range(CB_DEV):
            send_three[d, j] = sums[:, j * width:(j + 1) * width]
        copy = push(2, d, send_three.at[d], recv_three.at[d])
        copy.start()
        three.append(copy)
    sums_three = start_sums(2, row_squares(forward))
    back = terms(me)
    for d in range(1, n):
        three[d - 1].wait_recv()
        back = back + wide([recv_three[d, j].astype(f32) for j in range(CB_DEV)])
    beta_two = jnp.sqrt(end_sums(2, sums_three) + epsilon)
    cell_dir = back_one / alpha_one
    back_two = back / beta_two - beta_two * cell_dir

    sums_four = start_sums(3, row_squares(back_two))
    rho = jnp.sqrt(alpha_one * alpha_one + beta_two * beta_two)
    phi = alpha_one * beta_one / rho
    model = (phi / rho) * cell_dir
    for j in range(CB_DEV):
        model_ref[j] = model[:, j * width:(j + 1) * width]
    finish(one)
    finish(two)
    finish(three)
    finish(sums_one)
    finish(sums_two)
    finish(sums_three)
    alpha_two = jnp.sqrt(end_sums(3, sums_four) + epsilon)
    cell_next = back_two / alpha_two
    theta = beta_two * alpha_two / rho
    search = cells_root * (cell_next - (theta / rho) * cell_dir)
    for j in range(CB_DEV):
        search_ref[j] = search[:, j * width:(j + 1) * width]
    finish(sums_four)


def local(rhs_data, blocks, block_row, block_col):
    n = lax.axis_size("row")
    db, rows, width = rhs_data.shape
    count = blocks.shape[0]
    cells = CB_DEV * n
    vmem = pl.BlockSpec(memory_space=pltpu.VMEM)
    anywhere = pl.BlockSpec(memory_space=pltpu.HBM)
    strip = (cells, db * width, width)
    message = (CB_DEV, rows, width)
    strip_bytes = 2 * cells * db * width * width * 2
    strip_limit = max(LEAST, SPARE + 2 * strip_bytes + count * width * width * 2)
    exchange_limit = 2 * SPARE + strip_bytes
    high, low, send_one = pl.pallas_call(
        gather_kernel,
        out_shape=(
            jax.ShapeDtypeStruct(strip, bf16),
            jax.ShapeDtypeStruct(strip, bf16),
            jax.ShapeDtypeStruct((n,) + message, bf16),
        ),
        in_specs=[anywhere] * 3,
        out_specs=(vmem, vmem, vmem),
        scratch_shapes=[
            pltpu.SMEM((count,), jnp.int32),
            pltpu.VMEM((db, rows, width), f32),
            pltpu.VMEM((count, width, width), bf16),
            pltpu.VMEM((cells * db, width, width), f32),
            pltpu.SemaphoreType.DMA((2,)),
            pltpu.SemaphoreType.DMA((CHUNKS,)),
        ],
        compiler_params=pltpu.CompilerParams(vmem_limit_bytes=strip_limit),
        name="strip",
    )(block_col * db + block_row, rhs_data, blocks)
    out = jax.ShapeDtypeStruct((CB_DEV, rows, width), f32)
    return pl.pallas_call(
        functools.partial(exchange_kernel, n, math.sqrt(float(cells * width))),
        out_shape=(out, out),
        in_specs=[vmem, anywhere, vmem, vmem],
        out_specs=(vmem, vmem),
        scratch_shapes=[
            pltpu.VMEM((db, rows, width), f32),
            pltpu.VMEM((n,) + message, bf16),
            pltpu.VMEM(message, bf16),
            pltpu.VMEM((n,) + message, bf16),
            pltpu.VMEM((n,) + message, bf16),
            pltpu.VMEM((n,) + message, bf16),
            pltpu.VMEM((4, 1, width), f32),
            pltpu.VMEM((4, n, 1, width), f32),
            pltpu.SemaphoreType.DMA(()),
            pltpu.SemaphoreType.DMA((3, n)),
            pltpu.SemaphoreType.DMA((3, n)),
            pltpu.SemaphoreType.DMA((4, n)),
            pltpu.SemaphoreType.DMA((4, n)),
        ],
        compiler_params=pltpu.CompilerParams(
            collective_id=0, has_side_effects=True, vmem_limit_bytes=exchange_limit
        ),
        name="exchange",
    )(send_one, rhs_data, high, low)


def solution(mesh):
    in_specs = (
        P(("inv", "row"), None, None),
        P(("inv", "row"), None, None),
        P(("inv", "row")),
        P(("inv", "row")),
    )
    out_specs = (P(("inv", "row"), None, None), P(("inv", "row"), None, None))
    return jax.shard_map(local, mesh=mesh, in_specs=in_specs, out_specs=out_specs, check_vma=False)
```

time: 45.6 us -> 41.5 us (0.910)
  Pallas kernels: 41.3 us -> 38 us
  local copies, waits for them, and re-layouts: 3.29 us -> 1.93 us
  other arithmetic: 0 us -> 0.7 us
    pallas_call x1, Pallas kernels: 9.01 us -> 6.72 us  [local(): pl.pallas_call(gather_kernel, out_shape=(jax.ShapeDtypeStruct(strip, bf16...]
    unnamed x8 -> x4, local copies, waits for them, and re-layouts: 3.29 us -> 1.93 us
    pallas_call x1, Pallas kernels: 32.3 us -> 31.2 us  [local(): pl.pallas_call(functools.partial(exchange_kernel, n, math.sqrt(float(cell...]
    add x0 -> x1, other arithmetic: none -> 0.7 us  [local(): block_col * db + block_row]
where the time goes in v2:
time: 41.5 us; the launch traced here: 41.2 us
  Pallas kernels  38 us (92%)
  local copies, waits for them, and re-layouts  1.93 us (5%)
  other arithmetic  0.7 us (2%)
  between operations  0.65 us (2%)
    pallas_call x1, Pallas kernels, local(): pl.pallas_call(functools.partial(exchange_kernel, n, math.sqrt(float(cell...  31.2 us
    pallas_call x1, Pallas kernels, local(): pl.pallas_call(gather_kernel, out_shape=(jax.ShapeDtypeStruct(strip, bf16...  6.72 us
    unnamed x4, local copies, waits for them, and re-layouts  1.93 us

profile of v2, /device:TPU:0, one launch (start us, length us, event | category | flops | bytes accessed | tf_op | source)
XLA Modules:
  0.0 41.2 jit_solution(13260028065706607474)
XLA Ops:
  0.6 0.7 %multiply_add_fusion.place_hbm = s32[384]{0:T(512)S(1)} fusion(s32[384]{0:T(512)} %param.6, s32[384]{0:T(512)} %param.7), kind=kLoop, calls=%fused_computation | loop fusion | flops 768 | bytes 4608 | tf_op jit(solution)/shard_map/add | solution.py:294
  1.3 0.0 copy-start
  1.3 0.7 %copy-done = f32[2,16,128]{2,1,0:T(8,128)S(1)} copy-done((f32[2,16,128]{2,1,0:T(8,128)S(1)}, f32[2,16,128]{2,1,0:T(8,128)}, u32[]{:S(2)}) %copy-start) | copy-done | bytes 16408
  2.1 6.7 %strip.1 = (bf16[32,256,128]{2,1,0:T(8,128)(2,1)S(1)}, bf16[32,256,128]{2,1,0:T(8,128)(2,1)S(1)}, bf16[16,2,16,128]{3,2,1,0:T(8,128)(2,1)S(1)}) custom-call(s32[384]{0:T(512)S(1)} %multiply_add_fusion.place_hbm, f32[2,16,128]{2,1,0:T(8,128)S(1)} %copy-done, bf16[384,128,128]{2,1,0:T(8,128)(2,1)} %blocks_ref.1), custom_call_target="tpu_custom_call" | custom-call | tf_op jit(solution)/shard_map/strip/pallas_call | solution.py:275
  8.8 31.2 %exchange.1 = (f32[2,16,128]{2,1,0:T(8,128)S(1)}, f32[2,16,128]{2,1,0:T(8,128)S(1)}) custom-call(bf16[16,2,16,128]{3,2,1,0:T(8,128)(2,1)S(1)} %get-tuple-element.5.send_one, f32[2,16,128]{2,1,0:T(8,128)S(1)} %copy-done, bf16[32,256,128]{2,1,0:T(8,128)(2,1)S(1)} %get-tuple-element.6.high, bf16[32,256,128]{2,1,0:T(8,128)(2,1)S(1)} %get-tuple-element.7.low), custom_call_target="tpu_custom_call" | custom-call | tf_op jit(solution)/shard_map/exchange/pallas_call | solution.py:296
  40.0 0.6 %copy.8 = f32[2,16,128]{2,1,0:T(8,128)} copy(f32[2,16,128]{2,1,0:T(8,128)S(1)} %get-tuple-element.10) | data formatting | bytes 32768
  40.6 0.6 %copy.9 = f32[2,16,128]{2,1,0:T(8,128)} copy(f32[2,16,128]{2,1,0:T(8,128)S(1)} %get-tuple-element.11) | data formatting | bytes 32768
Async XLA Ops:
  1.3 0.7 %copy-start = (f32[2,16,128]{2,1,0:T(8,128)S(1)}, f32[2,16,128]{2,1,0:T(8,128)}, u32[]{:S(2)}) copy-start(f32[2,16,128]{2,1,0:T(8,128)} %rhs_hbm.3) | copy-start | bytes 49156

commit v3 on v2

--- a/solution.py
+++ b/solution.py
@@ -11,7 +11,6 @@
 CB_DEV = 2
 CHUNKS = 16
 SPARE = 4 * 1024 * 1024
-LEAST = 46 * 1024 * 1024
 
 epsilon = 1e-06
 bf16 = jnp.bfloat16
@@ -56,13 +55,15 @@
     return lax.dot_general(a, b, (((1,), (1,)), ((), ())), preferred_element_type=f32)
 
 
-def gather_kernel(
-    place_hbm, rhs_hbm, blocks_ref, high, low, send_ref,
-    place_ref, rhs_ref, held, total, small_sem, in_sem,
+def kernel(
+    n, cells_root, table_hbm, rhs_hbm, blocks_ref, model_ref, search_ref,
+    table, rhs_ref, held, total, high, low,
+    send_one, recv_one, send_two, recv_two, send_three, recv_three, send_sums, recv_sums,
+    small_sem, in_sem, send_sem, recv_sem, send_sum_sem, recv_sum_sem,
 ):
-    count, width = held.shape[0], held.shape[1]
-    db = rhs_ref.shape[0]
-    groups = send_ref.shape[0]
+    me = lax.axis_index("row")
+    db, rows, width = rhs_ref.shape
+    count = held.shape[0]
     chunk = count // CHUNKS
 
     def fetch(c):
@@ -70,7 +71,7 @@
         return pltpu.make_async_copy(blocks_ref.at[span], held.at[span], in_sem.at[c])
 
     small = [
-        pltpu.make_async_copy(place_hbm, place_ref, small_sem.at[0]),
+        pltpu.make_async_copy(table_hbm, table, small_sem.at[0]),
         pltpu.make_async_copy(rhs_hbm, rhs_ref, small_sem.at[1]),
     ]
     for copy in small:
@@ -78,63 +79,23 @@
     for c in range(CHUNKS):
         fetch(c).start()
 
-    def clear(p, carry):
-        total[p] = jnp.zeros((width, width), f32)
-        return carry
-
-    lax.fori_loop(0, total.shape[0], clear, 0)
-    for copy in small:
-        copy.wait()
-
-    for c in range(CHUNKS):
-        fetch(c).wait()
-
-        def add(k, carry):
-            total[place_ref[k]] += held[k].astype(f32)
-            return carry
-
-        lax.fori_loop(c * chunk, (c + 1) * chunk, add, 0, unroll=4)
-
-    data = jnp.concatenate([rhs_ref[b] for b in range(db)], axis=-1)
-    parts = stack_split(data)
-    rows = data.shape[0]
-
-    def product(s, carry):
-        tops, lows = [], []
-        for j in range(CB_DEV):
-            cell = s * CB_DEV + j
-            strip = jnp.concatenate([total[cell * db + b] for b in range(db)], axis=0)
-            top, rest = split_two(strip)
-            high[cell] = top
-            low[cell] = rest
-            tops.append(top)
-            lows.append(rest)
-        sums = dot(parts, jnp.concatenate(tops, axis=-1)) + dot(parts, jnp.concatenate(lows, axis=-1))
-        sums = sums[:rows] + sums[rows:]
-        for j in range(CB_DEV):
-            send_ref[s, j] = sums[:, j * width:(j + 1) * width].astype(bf16)
-        return carry
-
-    lax.fori_loop(0, groups, product, 0, unroll=2)
-
-
-def exchange_kernel(
-    n, cells_root, send_one, rhs_hbm, high, low, model_ref, search_ref,
-    rhs_ref, recv_one, send_two, recv_two, send_three, recv_three, send_sums, recv_sums,
-    load_sem, send_sem, recv_sem, send_sum_sem, recv_sum_sem,
-):
-    me = lax.axis_index("row")
-    width = rhs_ref.shape[2]
-    db = rhs_ref.shape[0]
-    rows = rhs_ref.shape[1]
-    small = pltpu.make_async_copy(rhs_hbm, rhs_ref, load_sem)
-    small.start()
     barrier = pltpu.get_barrier_semaphore()
     for d in range(1, n):
         pl.semaphore_signal(
             barrier, inc=1, device_id={"row": lax.rem(me + d, n)}, device_id_type=pl.DeviceIdType.MESH
         )
-    pl.semaphore_wait(barrier, n - 1)
+    total[count] = jnp.zeros((width, width), f32)
+    for copy in small:
+        copy.wait()
+
+    for c in range(CHUNKS):
+        fetch(c).wait()
+
+        def add(k, carry):
+            total[k] = total[table[k]] + held[k].astype(f32)
+            return carry
+
+        lax.fori_loop(c * chunk, (c + 1) * chunk, add, 0, unroll=4)
 
     def push(phase, d, src, dst):
         return pltpu.make_async_remote_copy(
@@ -183,11 +144,30 @@
     def wide(blocks):
         return jnp.concatenate(blocks, axis=-1)
 
+    data = wide([rhs_ref[b] for b in range(db)])
+    data_parts = stack_split(data)
+
+    def product(s, carry):
+        tops, lows = [], []
+        for j in range(CB_DEV):
+            cell = s * CB_DEV + j
+            dense = jnp.concatenate([total[table[count + cell * db + b]] for b in range(db)], axis=0)
+            top, rest = split_two(dense)
+            high[cell] = top
+            low[cell] = rest
+            tops.append(top)
+            lows.append(rest)
+        sums = dot(data_parts, wide(tops)) + dot(data_parts, wide(lows))
+        sums = sums[:rows] + sums[rows:]
+        for j in range(CB_DEV):
+            send_one[s, j] = sums[:, j * width:(j + 1) * width].astype(bf16)
+        return carry
+
+    lax.fori_loop(0, n, product, 0, unroll=2)
+    pl.semaphore_wait(barrier, n - 1)
     one = [push(0, d, send_one.at[to(d)], recv_one.at[d]) for d in range(1, n)]
     for copy in one:
         copy.start()
-    small.wait()
-    data = wide([rhs_ref[b] for b in range(db)])
     sums_one = start_sums(0, row_squares(data))
     mine = send_one[me].astype(f32)
     for d in range(1, n):
@@ -265,59 +245,53 @@
     db, rows, width = rhs_data.shape
     count = blocks.shape[0]
     cells = CB_DEV * n
+    place = block_col * db + block_row
+    k = jnp.arange(count, dtype=jnp.int32)
+    asked = jnp.concatenate([place, jnp.arange(cells * db, dtype=jnp.int32)])
+    before = jnp.concatenate([k, jnp.full((cells * db,), count, jnp.int32)])
+    hit = (place[None, :] == asked[:, None]) & (k[None, :] < before[:, None])
+    table = jnp.max(jnp.where(hit, k[None, :], -1), axis=1)
+    table = jnp.where(table < 0, count, table)
+
     vmem = pl.BlockSpec(memory_space=pltpu.VMEM)
     anywhere = pl.BlockSpec(memory_space=pltpu.HBM)
     strip = (cells, db * width, width)
     message = (CB_DEV, rows, width)
     strip_bytes = 2 * cells * db * width * width * 2
-    strip_limit = max(LEAST, SPARE + 2 * strip_bytes + count * width * width * 2)
-    exchange_limit = 2 * SPARE + strip_bytes
-    high, low, send_one = pl.pallas_call(
-        gather_kernel,
-        out_shape=(
-            jax.ShapeDtypeStruct(strip, bf16),
-            jax.ShapeDtypeStruct(strip, bf16),
-            jax.ShapeDtypeStruct((n,) + message, bf16),
-        ),
+    limit = SPARE + strip_bytes + 3 * count * width * width * 2
+    out = jax.ShapeDtypeStruct((CB_DEV, rows, width), f32)
+    return pl.pallas_call(
+        functools.partial(kernel, n, math.sqrt(float(cells * width))),
+        out_shape=(out, out),
         in_specs=[anywhere] * 3,
-        out_specs=(vmem, vmem, vmem),
+        out_specs=(vmem, vmem),
         scratch_shapes=[
-            pltpu.SMEM((count,), jnp.int32),
+            pltpu.SMEM(table.shape, jnp.int32),
             pltpu.VMEM((db, rows, width), f32),
             pltpu.VMEM((count, width, width), bf16),
-            pltpu.VMEM((cells * db, width, width), f32),
+            pltpu.VMEM((count + 1, width, width), f32),
+            pltpu.VMEM(strip, bf16),
+            pltpu.VMEM(strip, bf16),
+            pltpu.VMEM((n,) + message, bf16),
+            pltpu.VMEM((n,) + message, bf16),
+            pltpu.VMEM(message, bf16),
+            pltpu.VMEM((n,) + message, bf16),
+            pltpu.VMEM((n,) + message, bf16),
+            pltpu.VMEM((n,) + message, bf16),
+            pltpu.VMEM((4, 1, width), f32),
+            pltpu.VMEM((4, n, 1, width), f32),
             pltpu.SemaphoreType.DMA((2,)),
             pltpu.SemaphoreType.DMA((CHUNKS,)),
-        ],
-        compiler_params=pltpu.CompilerParams(vmem_limit_bytes=strip_limit),
-        name="strip",
-    )(block_col * db + block_row, rhs_data, blocks)
-    out = jax.ShapeDtypeStruct((CB_DEV, rows, width), f32)
-    return pl.pallas_call(
-        functools.partial(exchange_kernel, n, math.sqrt(float(cells * width))),
-        out_shape=(out, out),
-        in_specs=[vmem, anywhere, vmem, vmem],
-        out_specs=(vmem, vmem),
-        scratch_shapes=[
-            pltpu.VMEM((db, rows, width), f32),
-            pltpu.VMEM((n,) + message, bf16),
-            pltpu.VMEM(message, bf16),
-            pltpu.VMEM((n,) + message, bf16),
-            pltpu.VMEM((n,) + message, bf16),
-            pltpu.VMEM((n,) + message, bf16),
-            pltpu.VMEM((4, 1, width), f32),
-            pltpu.VMEM((4, n, 1, width), f32),
-            pltpu.SemaphoreType.DMA(()),
             pltpu.SemaphoreType.DMA((3, n)),
             pltpu.SemaphoreType.DMA((3, n)),
             pltpu.SemaphoreType.DMA((4, n)),
             pltpu.SemaphoreType.DMA((4, n)),
         ],
         compiler_params=pltpu.CompilerParams(
-            collective_id=0, has_side_effects=True, vmem_limit_bytes=exchange_limit
+            collective_id=0, has_side_effects=True, vmem_limit_bytes=limit
         ),
-        name="exchange",
-    )(send_one, rhs_data, high, low)
+        name="iteration",
+    )(table, rhs_data, blocks)
 
 
 def solution(mesh):

time: 41.5 us -> 38.5 us (0.928)
  Pallas kernels: 38 us -> 33.9 us
  other arithmetic: 0.7 us -> 1.68 us
    pallas_call x2 -> x1, Pallas kernels: 38 us -> 33.9 us  [local(): pl.pallas_call(functools.partial(kernel, n, math.sqrt(float(cells * width...]
    reduce_max x0 -> x1, other arithmetic: none -> 0.96 us  [local(): table = jnp.max(jnp.where(hit, k[None, :], -1), axis=1)]
where the time goes in v3:
time: 38.5 us; the launch traced here: 38.2 us
  Pallas kernels  33.9 us (88%)
  local copies, waits for them, and re-layouts  1.93 us (5%)
  other arithmetic  1.68 us (4%)
  between operations  0.66 us (2%)
    pallas_call x1, Pallas kernels, local(): pl.pallas_call(functools.partial(kernel, n, math.sqrt(float(cells * width...  33.9 us
    unnamed x4, local copies, waits for them, and re-layouts  1.93 us
    reduce_max x1, other arithmetic, local(): table = jnp.max(jnp.where(hit, k[None, :], -1), axis=1)  0.96 us

profile of v3, /device:TPU:0, one launch (start us, length us, event | category | flops | bytes accessed | tf_op | source)
XLA Modules:
  0.0 38.2 jit_solution(17351799829859091122)
XLA Ops:
  0.6 0.7 %multiply_add_fusion = s32[384]{0:T(512)S(1)} fusion(s32[384]{0:T(512)} %param.6, s32[384]{0:T(512)} %param.7), kind=kLoop, calls=%fused_computation.5 | loop fusion | flops 768 | bytes 4608 | tf_op jit(solution)/shard_map/add | solution.py:248
  1.4 1.0 %select_reduce_fusion = s32[448]{0:T(512)S(1)} fusion(s32[448]{0:T(512)} %constant.2.clone.1, s32[384]{0:T(512)S(1)} %multiply_add_fusion, s32[448]{0:T(512)S(1)} %pad_add_fusion), kind=kLoop, calls=%fused_computation | loop fusion | flops 859712 | bytes 6912 | tf_op jit(solution)/shard_map/reduce_max | solution.py:253
  2.3 0.0 copy-start
  2.3 0.7 %copy-done = f32[2,16,128]{2,1,0:T(8,128)S(1)} copy-done((f32[2,16,128]{2,1,0:T(8,128)S(1)}, f32[2,16,128]{2,1,0:T(8,128)}, u32[]{:S(2)}) %copy-start) | copy-done | bytes 16408
  3.1 33.9 %iteration.1 = (f32[2,16,128]{2,1,0:T(8,128)S(1)}, f32[2,16,128]{2,1,0:T(8,128)S(1)}) custom-call(s32[448]{0:T(512)S(1)} %compare_select_fusion.table_hbm, f32[2,16,128]{2,1,0:T(8,128)S(1)} %copy-done, bf16[384,128,128]{2,1,0:T(8,128)(2,1)} %blocks_ref.1), custom_call_target="tpu_custom_call" | custom-call | tf_op jit(solution)/shard_map/iteration/pallas_call | solution.py:263
  37.0 0.6 %copy.8 = f32[2,16,128]{2,1,0:T(8,128)} copy(f32[2,16,128]{2,1,0:T(8,128)S(1)} %get-tuple-element.4) | data formatting | bytes 32768
  37.6 0.6 %copy.9 = f32[2,16,128]{2,1,0:T(8,128)} copy(f32[2,16,128]{2,1,0:T(8,128)S(1)} %get-tuple-element.5) | data formatting | bytes 32768
  (3 shorter events, 0.0 us)
Async XLA Ops:
  2.3 0.7 %copy-start = (f32[2,16,128]{2,1,0:T(8,128)S(1)}, f32[2,16,128]{2,1,0:T(8,128)}, u32[]{:S(2)}) copy-start(f32[2,16,128]{2,1,0:T(8,128)} %rhs_hbm.1) | copy-start | bytes 49156

commit v4 on v3

--- a/solution.py
+++ b/solution.py
@@ -66,6 +66,16 @@
     count = held.shape[0]
     chunk = count // CHUNKS
 
+    def to(d):
+        index, bit = me, 1
+        while bit < n:
+            if d & bit:
+                index = index + bit * (1 - 2 * lax.rem(me // bit, 2))
+            bit *= 2
+        return index
+
+    far_first = range(n - 1, 0, -1)
+
     def fetch(c):
         span = pl.ds(c * chunk, chunk)
         return pltpu.make_async_copy(blocks_ref.at[span], held.at[span], in_sem.at[c])
@@ -82,7 +92,7 @@
     barrier = pltpu.get_barrier_semaphore()
     for d in range(1, n):
         pl.semaphore_signal(
-            barrier, inc=1, device_id={"row": lax.rem(me + d, n)}, device_id_type=pl.DeviceIdType.MESH
+            barrier, inc=1, device_id={"row": to(d)}, device_id_type=pl.DeviceIdType.MESH
         )
     total[count] = jnp.zeros((width, width), f32)
     for copy in small:
@@ -103,7 +113,7 @@
             dst_ref=dst,
             send_sem=send_sem.at[phase, d],
             recv_sem=recv_sem.at[phase, d],
-            device_id={"row": lax.rem(me + d, n)},
+            device_id={"row": to(d)},
             device_id_type=pl.DeviceIdType.MESH,
         )
 
@@ -113,13 +123,13 @@
             dst_ref=recv_sums.at[phase, d],
             send_sem=send_sum_sem.at[phase, d],
             recv_sem=recv_sum_sem.at[phase, d],
-            device_id={"row": lax.rem(me + d, n)},
+            device_id={"row": to(d)},
             device_id_type=pl.DeviceIdType.MESH,
         )
 
     def start_sums(phase, column):
         send_sums[phase] = to_lanes(column, width)
-        copies = [push_sums(phase, d) for d in range(1, n)]
+        copies = [push_sums(phase, d) for d in far_first]
         for copy in copies:
             copy.start()
         return copies
@@ -127,15 +137,9 @@
     def end_sums(phase, copies):
         line = send_sums[phase]
         for d in range(1, n):
-            copies[d - 1].wait_recv()
+            copies[n - 1 - d].wait_recv()
             line = line + recv_sums[phase, d]
         return from_lanes(line, rows)
-
-    def to(d):
-        return lax.rem(me + d, n)
-
-    def source(d):
-        return lax.rem(me + n - d, n)
 
     def finish(copies):
         for copy in copies:
@@ -147,7 +151,7 @@
     data = wide([rhs_ref[b] for b in range(db)])
     data_parts = stack_split(data)
 
-    def product(s, carry):
+    def product(s):
         tops, lows = [], []
         for j in range(CB_DEV):
             cell = s * CB_DEV + j
@@ -158,29 +162,29 @@
             tops.append(top)
             lows.append(rest)
         sums = dot(data_parts, wide(tops)) + dot(data_parts, wide(lows))
-        sums = sums[:rows] + sums[rows:]
+        return sums[:rows] + sums[rows:]
+
+    pl.semaphore_wait(barrier, n - 1)
+    sums_one = start_sums(0, row_squares(data))
+    one = {}
+    for d in far_first:
+        sums = product(to(d)).astype(bf16)
         for j in range(CB_DEV):
-            send_one[s, j] = sums[:, j * width:(j + 1) * width].astype(bf16)
-        return carry
-
-    lax.fori_loop(0, n, product, 0, unroll=2)
-    pl.semaphore_wait(barrier, n - 1)
-    one = [push(0, d, send_one.at[to(d)], recv_one.at[d]) for d in range(1, n)]
-    for copy in one:
-        copy.start()
-    sums_one = start_sums(0, row_squares(data))
-    mine = send_one[me].astype(f32)
+            send_one[d, j] = sums[:, j * width:(j + 1) * width]
+        one[d] = push(0, d, send_one.at[d], recv_one.at[d])
+        one[d].start()
+    mine = product(me)
     for d in range(1, n):
-        one[d - 1].wait_recv()
-        mine = mine + recv_one[d].astype(f32)
+        one[d].wait_recv()
+        mine = mine + wide([recv_one[d, j].astype(f32) for j in range(CB_DEV)])
     beta_one = jnp.sqrt(end_sums(0, sums_one) + epsilon)
-    back_one = wide([mine[j] for j in range(CB_DEV)]) / beta_one
+    back_one = mine / beta_one
 
     back_bf = back_one.astype(bf16)
     for j in range(CB_DEV):
         send_two[j] = back_bf[:, j * width:(j + 1) * width]
-    two = [push(1, d, send_two, recv_two.at[d]) for d in range(1, n)]
-    for copy in two:
+    two = {d: push(1, d, send_two, recv_two.at[d]) for d in far_first}
+    for copy in two.values():
         copy.start()
     sums_two = start_sums(1, row_squares(back_one))
 
@@ -189,8 +193,8 @@
 
     forward = dot_t(back_bf, strip(high, me)) + dot_t(back_bf, strip(low, me))
     for d in range(1, n):
-        two[d - 1].wait_recv()
-        s = source(d)
+        two[d].wait_recv()
+        s = to(d)
         cells = wide([recv_two[d, j] for j in range(CB_DEV)])
         forward = forward + dot_t(cells, strip(high, s)) + dot_t(cells, strip(low, s))
     alpha_one = jnp.sqrt(end_sums(1, sums_two) + epsilon)
@@ -202,18 +206,17 @@
         sums = dot(parts, strip(high, s)) + dot(parts, strip(low, s))
         return sums[:rows] + sums[rows:]
 
-    three = []
-    for d in range(1, n):
+    sums_three = start_sums(2, row_squares(forward))
+    three = {}
+    for d in far_first:
         sums = terms(to(d)).astype(bf16)
         for j in range(CB_DEV):
             send_three[d, j] = sums[:, j * width:(j + 1) * width]
-        copy = push(2, d, send_three.at[d], recv_three.at[d])
-        copy.start()
-        three.append(copy)
-    sums_three = start_sums(2, row_squares(forward))
+        three[d] = push(2, d, send_three.at[d], recv_three.at[d])
+        three[d].start()
     back = terms(me)
     for d in range(1, n):
-        three[d - 1].wait_recv()
+        three[d].wait_recv()
         back = back + wide([recv_three[d, j].astype(f32) for j in range(CB_DEV)])
     beta_two = jnp.sqrt(end_sums(2, sums_three) + epsilon)
     cell_dir = back_one / alpha_one
@@ -225,9 +228,9 @@
     model = (phi / rho) * cell_dir
     for j in range(CB_DEV):
         model_ref[j] = model[:, j * width:(j + 1) * width]
-    finish(one)
-    finish(two)
-    finish(three)
+    finish(one.values())
+    finish(two.values())
+    finish(three.values())
     finish(sums_one)
     finish(sums_two)
     finish(sums_three)

time: 38.5 us -> 36.4 us (0.945)
  Pallas kernels: 33.9 us -> 31.8 us
    pallas_call x1, Pallas kernels: 33.9 us -> 31.8 us  [local(): pl.pallas_call(functools.partial(kernel, n, math.sqrt(float(cells * width...]
where the time goes in v4:
time: 36.4 us; the launch traced here: 36.1 us
  Pallas kernels  31.8 us (87%)
  local copies, waits for them, and re-layouts  1.93 us (5%)
  other arithmetic  1.68 us (5%)
  between operations  0.66 us (2%)
    pallas_call x1, Pallas kernels, local(): pl.pallas_call(functools.partial(kernel, n, math.sqrt(float(cells * width...  31.8 us
    unnamed x4, local copies, waits for them, and re-layouts  1.93 us
    reduce_max x1, other arithmetic, local(): table = jnp.max(jnp.where(hit, k[None, :], -1), axis=1)  0.96 us

profile of v4, /device:TPU:0, one launch (start us, length us, event | category | flops | bytes accessed | tf_op | source)
XLA Modules:
  0.0 36.1 jit_solution(17884920448116491937)
XLA Ops:
  0.6 0.7 %multiply_add_fusion = s32[384]{0:T(512)S(1)} fusion(s32[384]{0:T(512)} %param.6, s32[384]{0:T(512)} %param.7), kind=kLoop, calls=%fused_computation.5 | loop fusion | flops 768 | bytes 4608 | tf_op jit(solution)/shard_map/add | solution.py:251
  1.4 1.0 %select_reduce_fusion = s32[448]{0:T(512)S(1)} fusion(s32[448]{0:T(512)} %constant.2.clone.1, s32[384]{0:T(512)S(1)} %multiply_add_fusion, s32[448]{0:T(512)S(1)} %pad_add_fusion), kind=kLoop, calls=%fused_computation | loop fusion | flops 859712 | bytes 6912 | tf_op jit(solution)/shard_map/reduce_max | solution.py:256
  2.3 0.0 copy-start
  2.3 0.7 %copy-done = f32[2,16,128]{2,1,0:T(8,128)S(1)} copy-done((f32[2,16,128]{2,1,0:T(8,128)S(1)}, f32[2,16,128]{2,1,0:T(8,128)}, u32[]{:S(2)}) %copy-start) | copy-done | bytes 16408
  3.1 31.8 %iteration.1 = (f32[2,16,128]{2,1,0:T(8,128)S(1)}, f32[2,16,128]{2,1,0:T(8,128)S(1)}) custom-call(s32[448]{0:T(512)S(1)} %compare_select_fusion.table_hbm, f32[2,16,128]{2,1,0:T(8,128)S(1)} %copy-done, bf16[384,128,128]{2,1,0:T(8,128)(2,1)} %blocks_ref.1), custom_call_target="tpu_custom_call" | custom-call | tf_op jit(solution)/shard_map/iteration/pallas_call | solution.py:266
  34.9 0.6 %copy.8 = f32[2,16,128]{2,1,0:T(8,128)} copy(f32[2,16,128]{2,1,0:T(8,128)S(1)} %get-tuple-element.4) | data formatting | bytes 32768
  35.5 0.6 %copy.9 = f32[2,16,128]{2,1,0:T(8,128)} copy(f32[2,16,128]{2,1,0:T(8,128)S(1)} %get-tuple-element.5) | data formatting | bytes 32768
  (3 shorter events, 0.0 us)
Async XLA Ops:
  2.3 0.7 %copy-start = (f32[2,16,128]{2,1,0:T(8,128)S(1)}, f32[2,16,128]{2,1,0:T(8,128)}, u32[]{:S(2)}) copy-start(f32[2,16,128]{2,1,0:T(8,128)} %rhs_hbm.1) | copy-start | bytes 49156

commit v5 on v4

--- a/solution.py
+++ b/solution.py
@@ -56,7 +56,7 @@
 
 
 def kernel(
-    n, cells_root, table_hbm, rhs_hbm, blocks_ref, model_ref, search_ref,
+    n, table_hbm, rhs_hbm, blocks_ref, model_ref, search_ref, factor_ref,
     table, rhs_ref, held, total, high, low,
     send_one, recv_one, send_two, recv_two, send_three, recv_three, send_sums, recv_sums,
     small_sem, in_sem, send_sem, recv_sem, send_sum_sem, recv_sum_sem,
@@ -102,7 +102,7 @@
         fetch(c).wait()
 
         def add(k, carry):
-            total[k] = total[table[k]] + held[k].astype(f32)
+            total[k] = total[table[0, k]] + held[k].astype(f32)
             return carry
 
         lax.fori_loop(c * chunk, (c + 1) * chunk, add, 0, unroll=4)
@@ -155,7 +155,7 @@
         tops, lows = [], []
         for j in range(CB_DEV):
             cell = s * CB_DEV + j
-            dense = jnp.concatenate([total[table[count + cell * db + b]] for b in range(db)], axis=0)
+            dense = jnp.concatenate([total[table[1, cell * db + b]] for b in range(db)], axis=0)
             top, rest = split_two(dense)
             high[cell] = top
             low[cell] = rest
@@ -227,7 +227,7 @@
     phi = alpha_one * beta_one / rho
     model = (phi / rho) * cell_dir
     for j in range(CB_DEV):
-        model_ref[j] = model[:, j * width:(j + 1) * width]
+        model_ref[j] = cell_dir[:, j * width:(j + 1) * width]
     finish(one.values())
     finish(two.values())
     finish(three.values())
@@ -237,9 +237,10 @@
     alpha_two = jnp.sqrt(end_sums(3, sums_four) + epsilon)
     cell_next = back_two / alpha_two
     theta = beta_two * alpha_two / rho
-    search = cells_root * (cell_next - (theta / rho) * cell_dir)
     for j in range(CB_DEV):
-        search_ref[j] = search[:, j * width:(j + 1) * width]
+        search_ref[j] = cell_next[:, j * width:(j + 1) * width]
+    factor_ref[0] = jnp.broadcast_to(phi / rho, (rows, width))
+    factor_ref[1] = jnp.broadcast_to(theta / rho, (rows, width))
     finish(sums_four)
 
 
@@ -250,10 +251,13 @@
     cells = CB_DEV * n
     place = block_col * db + block_row
     k = jnp.arange(count, dtype=jnp.int32)
-    asked = jnp.concatenate([place, jnp.arange(cells * db, dtype=jnp.int32)])
-    before = jnp.concatenate([k, jnp.full((cells * db,), count, jnp.int32)])
-    hit = (place[None, :] == asked[:, None]) & (k[None, :] < before[:, None])
-    table = jnp.max(jnp.where(hit, k[None, :], -1), axis=1)
+    slots = max(count, cells * db)
+    asked = jnp.pad(place, (0, slots - count), constant_values=-1)
+    slot = jnp.arange(slots, dtype=jnp.int32)
+    earlier = (place[None, :] == asked[:, None]) & (k[None, :] < slot[:, None])
+    here = place[None, :] == slot[:, None]
+    hit = jnp.stack([earlier, here])
+    table = jnp.max(jnp.where(hit, k[None, None, :], -1), axis=2)
     table = jnp.where(table < 0, count, table)
 
     vmem = pl.BlockSpec(memory_space=pltpu.VMEM)
@@ -263,11 +267,11 @@
     strip_bytes = 2 * cells * db * width * width * 2
     limit = SPARE + strip_bytes + 3 * count * width * width * 2
     out = jax.ShapeDtypeStruct((CB_DEV, rows, width), f32)
-    return pl.pallas_call(
-        functools.partial(kernel, n, math.sqrt(float(cells * width))),
-        out_shape=(out, out),
+    cell_dir, cell_next, factors = pl.pallas_call(
+        functools.partial(kernel, n),
+        out_shape=(out, out, jax.ShapeDtypeStruct((2, rows, width), f32)),
         in_specs=[anywhere] * 3,
-        out_specs=(vmem, vmem),
+        out_specs=(vmem, vmem, vmem),
         scratch_shapes=[
             pltpu.SMEM(table.shape, jnp.int32),
             pltpu.VMEM((db, rows, width), f32),
@@ -295,6 +299,10 @@
         ),
         name="iteration",
     )(table, rhs_data, blocks)
+    scale = jnp.float32(math.sqrt(float(cells * width)))
+    model_update = factors[0][None] * cell_dir
+    next_search = scale * (cell_next - factors[1][None] * cell_dir)
+    return model_update, next_search
 
 
 def solution(mesh):

time: 36.4 us -> 35.2 us (0.967)
  local copies, waits for them, and re-layouts: 1.93 us -> 0.72 us
    unnamed x4 -> x2, local copies, waits for them, and re-layouts: 1.93 us -> 0.71 us
    reduce_max x1, other arithmetic: 0.96 us -> 0.26 us  [local(): table = jnp.max(jnp.where(hit, k[None, None, :], -1), axis=2)]
    mul x0 -> x1, other arithmetic: none -> 0.62 us  [local(): next_search = scale * (cell_next - factors[1][None] * cell_dir)]
where the time goes in v5:
time: 35.2 us; the launch traced here: 35 us
  Pallas kernels  31.8 us (90%)
  other arithmetic  1.76 us (5%)
  local copies, waits for them, and re-layouts  0.72 us (2%)
  between operations  0.66 us (2%)
    pallas_call x1, Pallas kernels, local(): pl.pallas_call(functools.partial(kernel, n), out_shape=(out, out, jax.Sha...  31.8 us
    unnamed x2, local copies, waits for them, and re-layouts  0.71 us

profile of v5, /device:TPU:0, one launch (start us, length us, event | category | flops | bytes accessed | tf_op | source)
XLA Modules:
  0.0 35.0 jit_solution(2398244718654230331)
XLA Ops:
  0.6 0.7 %multiply_add_fusion = s32[384]{0:T(512)S(1)} fusion(s32[384]{0:T(512)} %param.6, s32[384]{0:T(512)} %param.7), kind=kLoop, calls=%fused_computation.9 | loop fusion | flops 768 | bytes 4608 | tf_op jit(solution)/shard_map/add | solution.py:252
  1.3 0.2 fusion
  1.5 0.3 select_reduce_fusion
  1.8 0.0 copy-start
  1.8 0.7 %copy-done = f32[2,16,128]{2,1,0:T(8,128)S(1)} copy-done((f32[2,16,128]{2,1,0:T(8,128)S(1)}, f32[2,16,128]{2,1,0:T(8,128)}, u32[]{:S(2)}) %copy-start) | copy-done | bytes 16408
  2.5 31.8 %iteration.1 = (f32[2,16,128]{2,1,0:T(8,128)S(1)}, f32[2,16,128]{2,1,0:T(8,128)S(1)}, f32[2,16,128]{2,1,0:T(8,128)S(1)}) custom-call(s32[2,384]{1,0:T(2,128)S(1)} %compare_select_fusion.table_hbm, f32[2,16,128]{2,1,0:T(8,128)S(1)} %copy-done, bf16[384,128,128]{2,1,0:T(8,128)(2,1)} %blocks_ref.1), custom_call_target="tpu_custom_call" | custom-call | tf_op jit(solution)/shard_map/iteration/pallas_call | solution.py:270
  34.3 0.6 %subtract_multiply_fusion = (f32[2,16,128]{2,1,0:T(8,128)}, f32[2,16,128]{2,1,0:T(8,128)}) fusion(f32[2,16,128]{2,1,0:T(8,128)S(1)} %get-tuple-element.7, f32[2,16,128]{2,1,0:T(8,128)S(1)} %get-tuple-element.6, f32[16,128]{1,0:T(8,128)S(1)} %get-tuple-element.10, f32[16,128]{1,0:T(8,128)S(1)} %get-tuple-element.11), kind=kLoop, calls=%fused_computation.4 | loop fusion | flops 16384 | bytes 81920 | tf_op jit(solution)/shard_map/mul | solution.py:304
  (2 shorter events, 0.0 us)
Async XLA Ops:
  1.8 0.7 %copy-start = (f32[2,16,128]{2,1,0:T(8,128)S(1)}, f32[2,16,128]{2,1,0:T(8,128)}, u32[]{:S(2)}) copy-start(f32[2,16,128]{2,1,0:T(8,128)} %rhs_hbm.1) | copy-start | bytes 49156
